TPU v7x, 1024 devices: a whole 4x4x32 slice. The times are simulated.
1024 devices in a mesh: space: 128 (over z, x), blk: 8 (over y, core).
Axes of the slice: x: 4, y: 4, z: 32, core: 2. Of those that a mesh axis runs over, the one named last changes fastest.
Arguments:
- snapshots: float32 [1024, 16, 16, 1024], P('space', None, None, 'blk'), may hold values from -40 to 40, as said below
Outputs:
- rotated: float32 [1024, 16, 16, 1024], P('space', None, None, 'blk')
Inputs may be any that keep to these rules, and one draw needn't show every extreme that they name: `snapshots`: snapshot values are finite reals.
All inputs are finite; a program needn't handle non-finite values.
Results may differ from a plain program's by a relative error of at most 0.0003.
Values sent between devices are 32-bit elements; how exact they have to be, the bound alone decides.
A program may use at most 32 MiB of HBM per device.

v0:
```python
import jax
import jax.numpy as jnp
from jax import lax
from jax.sharding import PartitionSpec as P

ROUNDS = 2


def padded_2(shard, sides, width):
    for axis, dim in sides:
        size, length = (lax.axis_size(axis), shard.shape[dim])
        up = [(i, (i + 1) % size) for i in range(size - 1)]
        down = [(j, i) for i, j in up]
        last = lax.slice_in_dim(shard, length - width, length, axis=dim)
        first = lax.slice_in_dim(shard, 0, width, axis=dim)
        before = lax.ppermute(last, axis, up)
        after = lax.ppermute(first, axis, down)
        shard = jnp.concatenate([before, shard, after], axis=dim)
    return shard


def from_partner(block, axis, stride):
    count = lax.axis_size(axis)
    route = []
    for low in range(count):
        high = low | 1 << stride
        if high != low and high < count:
            route += [(low, high), (high, low)]
    return lax.ppermute(block, axis, route)


def weighted(block):
    padded = padded_2(block, (("space", 0),), 1)
    layers = block.shape[0]
    cells_y = block.shape[1]
    cells_z = block.shape[2]
    sides = jnp.pad(block, ((0, 0), (1, 1), (1, 1), (0, 0)))
    near = padded[2:] + padded[:-2]
    near = near + sides[:, 2:, 1:-1] + sides[:, :-2, 1:-1]
    near = near + sides[:, 1:-1, 2:] + sides[:, 1:-1, :-2]
    total_x = layers * lax.axis_size("space")
    pos_x = lax.axis_index("space") * layers + jnp.arange(layers, dtype=jnp.int32)
    pos_y = jnp.arange(cells_y, dtype=jnp.int32)
    pos_z = jnp.arange(cells_z, dtype=jnp.int32)
    deg_x = (pos_x > 0).astype(jnp.float32) + (pos_x < total_x - 1).astype(jnp.float32)
    deg_y = (pos_y > 0).astype(jnp.float32) + (pos_y < cells_y - 1).astype(jnp.float32)
    deg_z = (pos_z > 0).astype(jnp.float32) + (pos_z < cells_z - 1).astype(jnp.float32)
    degree = deg_x[:, None, None] + deg_y[None, :, None] + deg_z[None, None, :]
    return block + (degree[..., None] * block - near)


def gram_of(left, right):
    width = left.shape[-1]
    return lax.dot_general(
        left.reshape(-1, width),
        right.reshape(-1, width),
        (((0,), (0,)), ((), ())),
        precision=lax.Precision.HIGHEST,
        preferred_element_type=jnp.float32,
    )


def rotation(own_diag, peer_diag, cross, parity):
    denom = jnp.diagonal(own_diag)[:, None] + jnp.diagonal(peer_diag)[None, :]
    ratios = cross / denom
    eye_mat = jnp.eye(cross.shape[0], dtype=jnp.float32)
    normal_mat = eye_mat + jnp.dot(
        ratios, ratios.T, precision=lax.Precision.HIGHEST, preferred_element_type=jnp.float32
    )
    factor = jnp.linalg.cholesky(normal_mat)
    inverse = jax.scipy.linalg.cho_solve((factor, True), eye_mat)
    solved = jax.scipy.linalg.cho_solve((factor, True), ratios)
    keep_mat = 2.0 * inverse - eye_mat
    take_mat = 2.0 * parity * solved.T
    return (keep_mat, take_mat)


def mix_blocks(own_block, peer_block, keep_mat, take_mat):
    width = own_block.shape[-1]
    first = jnp.dot(
        own_block.reshape(-1, width),
        keep_mat,
        precision=lax.Precision.HIGHEST,
        preferred_element_type=jnp.float32,
    )
    second = jnp.dot(
        peer_block.reshape(-1, width),
        take_mat,
        precision=lax.Precision.HIGHEST,
        preferred_element_type=jnp.float32,
    )
    return (first + second).reshape(own_block.shape)


def shards(snapshots):
    own_block = snapshots
    for sweep_round in range(ROUNDS):
        parity = ((lax.axis_index("blk") >> sweep_round & 1) * 2 - 1).astype(jnp.float32)
        outgoing = own_block
        incoming = from_partner(outgoing, "blk", sweep_round)
        image = weighted(own_block)
        local_diag = gram_of(image, own_block)
        local_cross = gram_of(image, incoming)
        own_diag, cross = lax.psum((local_diag, local_cross), "space")
        peer_diag = from_partner(own_diag, "blk", sweep_round)
        keep_mat, take_mat = rotation(own_diag, peer_diag, cross, parity)
        own_block = mix_blocks(own_block, incoming, keep_mat, take_mat)
    return own_block


def solution(mesh):
    return jax.shard_map(
        shards,
        mesh=mesh,
        in_specs=(P("space", None, None, "blk"),),
        out_specs=P("space", None, None, "blk"),
        check_vma=False,
    )
```

profile of v0, /device:TPU:1, one launch (start us, length us, event | category | flops | bytes accessed | tf_op | source)
XLA Modules:
  0.0 1107.6 jit_solution(6208259608134355628)
XLA Ops:
  6.5 16.1 %collective-permute-start.2 = (f32[8,16,16,128]{3,2,1,0:T(8,128)}, f32[8,16,16,128]{3,2,1,0:T(8,128)S(1)}, u32[]{:S(2)}, u32[]{:S(2)}) collective-permute-start(f32[8,16,16,128]{3,2,1,0:T(8,128)} %param.4), channel_id=1, source_target_pairs={{0,1},{1,0},{2,3},{3,2},{4,5},{5,4},{6,7},{7,6},{8,9},{9,8},{10,11... | collective-permute-start | bytes 3145736 | tf_op jit(solution)/shard_map/ppermute | solution.py:29
  22.6 1.0 fusion.37
  23.6 1.3 collective-permute-start.1
  24.9 1.3 collective-permute-start
  26.4 1.6 collective-permute-done.1
  28.0 3.9 collective-permute-done
  31.9 5.4 fusion.7
  37.3 2.5 convolution_bitcast_fusion.1
  39.8 2.5 convolution_bitcast_fusion.2
  42.4 475.3 %all-reduce.9.cloned.1.call-done = (f32[128,128]{1,0:T(8,128)}, f32[128,128]{1,0:T(8,128)}) async-done(((f32[128,128]{1,0:T(8,128)}, f32[128,128]{1,0:T(8,128)}), (f32[128,128]{1,0:T(8,128)}, f32[128,128]{1,0:T(8,128)})) %all-reduce.9.cloned.1.call-update) | async-done | bytes 131088 | tf_op jit(solution)/shard_map/psum | solution.py:104
  517.7 24.5 %collective-permute-start.3 = (f32[128,128]{1,0:T(8,128)}, f32[128,128]{1,0:T(8,128)S(1)}, u32[]{:S(2)}, u32[]{:S(2)}) collective-permute-start(f32[128,128]{1,0:T(8,128)} %get-tuple-element.10), channel_id=1, source_target_pairs={{0,1},{1,0},{2,3},{3,2},{4,5},{5,4},{6,7},{7,6},{8,9},{9,8},{10,11... | collective-permute-start | bytes 196616 | tf_op jit(solution)/shard_map/ppermute | solution.py:29
  542.2 1.9 gather_fusion
  544.1 1.2 gather_fusion.1
  545.4 0.3 convolution_add_fusion.3
  545.9 11.7 %cholesky.44 = f32[128,128]{1,0:T(8,128)S(1)} custom-call(f32[128,128]{1,0:T(8,128)S(1)} %fusion.33), custom_call_target="Cholesky" | custom-call | tf_op jit(solution)/shard_map/jit(cholesky)/cholesky | solution.py:70
  557.6 0.6 compare_reduce_fusion.1
  558.3 0.7 fusion.20
  558.9 9.8 custom-call.18
  569.0 0.3 fusion.29
  569.4 0.3 fusion.1
  569.7 1.0 fusion.38
  570.9 1.1 convolution_add_fusion.1
  572.0 0.3 copy.16
  572.3 3.1 collective-permute-start.6
  575.4 0.8 copy.18
  576.2 2.3 collective-permute-start.5
  578.5 0.7 copy.17
  579.2 1.5 collective-permute-start.4
  580.7 0.6 collective-permute-done.5
  581.4 4.4 collective-permute-done.4
  585.8 0.5 fusion.13
  586.2 2.5 fusion.39
  588.7 10.2 collective-permute-done.6
  599.0 2.5 convolution_bitcast_fusion
  601.5 464.1 %all-reduce.7.cloned.1.call-done = (f32[128,128]{1,0:T(8,128)}, f32[128,128]{1,0:T(8,128)}) async-done(((f32[128,128]{1,0:T(8,128)}, f32[128,128]{1,0:T(8,128)}), (f32[128,128]{1,0:T(8,128)}, f32[128,128]{1,0:T(8,128)})) %all-reduce.7.cloned.1.call-update) | async-done | bytes 131088 | tf_op jit(solution)/shard_map/psum | solution.py:104
  1065.6 3.2 collective-permute-start.7
  1068.8 1.9 gather_fusion.2
  1070.8 0.6 collective-permute-done.7
  1071.3 1.2 gather_fusion.3
  1072.6 0.3 convolution_add_fusion.2
  1073.0 11.7 %cholesky.55 = f32[128,128]{1,0:T(8,128)S(1)} custom-call(f32[128,128]{1,0:T(8,128)S(1)} %fusion.27), custom_call_target="Cholesky" | custom-call | tf_op jit(solution)/shard_map/jit(cholesky)/cholesky | solution.py:70
  1084.8 0.6 compare_reduce_fusion
  1085.4 0.7 fusion.21
  1086.1 9.8 custom-call.20
  1096.2 0.3 fusion.23
  1096.5 0.3 fusion
  1096.8 1.8 fusion.40
  1098.9 2.0 convolution_add_fusion
  (28 shorter events, 1.6 us)
Async XLA Ops:
  6.5 511.1 %all-reduce.9.cloned.1.call-start = ((), (), s32[]{:S(2)}) async-start(), calls=%async_computation.1 | async-start | bytes 262144 | tf_op jit(solution)/shard_map/psum | solution.py:104
  6.5 33.2 %collective-permute-start.2 = (f32[8,16,16,128]{3,2,1,0:T(8,128)}, f32[8,16,16,128]{3,2,1,0:T(8,128)S(1)}, u32[]{:S(2)}, u32[]{:S(2)}) collective-permute-start(f32[8,16,16,128]{3,2,1,0:T(8,128)} %param.4), channel_id=1, source_target_pairs={{0,1},{1,0},{2,3},{3,2},{4,5},{5,4},{6,7},{7,6},{8,9},{9,8},{10,11... | collective-permute-start | bytes 3145736 | tf_op jit(solution)/shard_map/ppermute | solution.py:29
  23.6 4.4 collective-permute-start.1
  24.9 7.0 collective-permute-start
  26.4 10.9 copy-start
  42.3 1023.3 %all-reduce.7.cloned.1.call-start = ((), (), s32[]{:S(2)}) async-start(), calls=%async_computation | async-start | bytes 262144 | tf_op jit(solution)/shard_map/psum | solution.py:104
  517.7 27.7 %copy-start.1 = (f32[128,128]{1,0:T(8,128)S(1)}, f32[128,128]{1,0:T(8,128)}, u32[]{:S(2)}) copy-start(f32[128,128]{1,0:T(8,128)} %get-tuple-element.9) | copy-start | bytes 196612
  517.7 26.5 %collective-permute-start.3 = (f32[128,128]{1,0:T(8,128)}, f32[128,128]{1,0:T(8,128)S(1)}, u32[]{:S(2)}, u32[]{:S(2)}) collective-permute-start(f32[128,128]{1,0:T(8,128)} %get-tuple-element.10), channel_id=1, source_target_pairs={{0,1},{1,0},{2,3},{3,2},{4,5},{5,4},{6,7},{7,6},{8,9},{9,8},{10,11... | collective-permute-start | bytes 196616 | tf_op jit(solution)/shard_map/ppermute | solution.py:29
  572.3 26.7 %collective-permute-start.6 = (f32[8,16,16,128]{3,2,1,0:T(8,128)S(1)}, f32[8,16,16,128]{3,2,1,0:T(8,128)S(1)}, u32[]{:S(2)}, u32[]{:S(2)}) collective-permute-start(f32[8,16,16,128]{3,2,1,0:T(8,128)S(1)} %bitcast.80), channel_id=1, source_target_pairs={{0,2},{2,0},{1,3},{3,1},{4,6},{6,4},{5,7},{7,5},{8,10},{10,8},{9,1... | collective-permute-start | bytes 3145736 | tf_op jit(solution)/shard_map/ppermute | solution.py:29
  576.2 5.1 collective-permute-start.5
  579.2 6.6 collective-permute-start.4
  1065.6 7.0 copy-start.2
  1065.6 5.7 collective-permute-start.7
Sparse Core Ops, SparseCore 0:
  42.4 475.1 all-reduce.8
  601.6 463.8 all-reduce.6
where the time goes:
time: 1130 us; the launch traced here: 1110 us
  waiting for transfers between devices  961 us (85%)
  starting transfers between devices  53.3 us (5%)
  other arithmetic  51.7 us (5%)
  matrix products  18.7 us (2%)
  between operations  13.7 us (1%)
    psum x2, waiting for transfers between devices, shards(): own_diag, cross = lax.psum((local_diag, local_cross), 'space')  939 us
    ppermute x4, starting transfers between devices, from_partner(): return lax.ppermute(block, axis, route)  46.9 us
    another operation x6, other arithmetic, rotation(): factor = jnp.linalg.cholesky(normal_mat)  24.8 us
  transfers between devices with their start and end apart: 10, of which 8 were waited for; matrix products, arithmetic and copies ran while one was open for 2% of the time, Pallas kernels for 0%

commit v1 on v0

--- a/solution.py
+++ b/solution.py
@@ -1,9 +1,99 @@
+import functools
+
 import jax
 import jax.numpy as jnp
 from jax import lax
+from jax.experimental import pallas as pl
+from jax.experimental.pallas import tpu as pltpu
 from jax.sharding import PartitionSpec as P
 
 ROUNDS = 2
+NXC = 4
+MESH = pl.DeviceIdType.MESH
+
+
+def sum_kernel(nz, in_ref, out_ref, rx, part, rz, gz, send, recv):
+    space = lax.axis_index("space")
+    blk = lax.axis_index("blk")
+    z, x = space // NXC, space % NXC
+    rows = rx.shape[1]
+
+    def x_peer(d):
+        return z * NXC + (x + d) % NXC
+
+    def z_peer(d):
+        return ((z + d) % nz) * NXC + x
+
+    def remote(src, dst, phase, peer):
+        return pltpu.make_async_remote_copy(
+            src_ref=src,
+            dst_ref=dst,
+            send_sem=send.at[phase],
+            recv_sem=recv.at[phase],
+            device_id=(peer, blk),
+            device_id_type=MESH,
+        )
+
+    def wait_bytes(ref, phase):
+        pltpu.make_async_copy(ref, ref, recv.at[phase]).wait()
+        pltpu.make_async_copy(ref, ref, send.at[phase]).wait()
+
+    barrier = pltpu.get_barrier_semaphore()
+    for d in range(1, NXC):
+        pl.semaphore_signal(barrier, inc=1, device_id=(x_peer(d), blk), device_id_type=MESH)
+
+    @pl.loop(1, nz)
+    def _(d):
+        pl.semaphore_signal(barrier, inc=1, device_id=(z_peer(d), blk), device_id_type=MESH)
+
+    pl.semaphore_wait(barrier, NXC - 1 + nz - 1)
+
+    def own_rows(index):
+        return pl.ds(pl.multiple_of(index * rows, rows), rows)
+
+    for d in range(1, NXC):
+        remote(in_ref.at[own_rows((x + d) % NXC)], rx.at[d - 1], 0, x_peer(d)).start()
+    wait_bytes(rx, 0)
+    mine = in_ref[own_rows(x)] + rx[0] + rx[1] + rx[2]
+    part[...] = mine.reshape(part.shape)
+
+    @pl.loop(1, nz)
+    def _(d):
+        remote(part.at[(z + d) % nz], rz.at[d - 1], 1, z_peer(d)).start()
+
+    wait_bytes(rz, 1)
+    gz[pl.ds(z, 1)] = part[pl.ds(z, 1)] + jnp.sum(rz[...], axis=0, keepdims=True)
+
+    @pl.loop(1, nz)
+    def _(d):
+        remote(gz.at[z], gz.at[z], 2, z_peer(d)).start()
+
+    wait_bytes(rz, 2)
+    out_ref[own_rows(x)] = gz[...].reshape(rows, gz.shape[-1])
+    for d in range(1, NXC):
+        remote(out_ref.at[own_rows(x)], out_ref.at[own_rows(x)], 3, x_peer(d)).start()
+    wait_bytes(rx, 3)
+
+
+def sum_over_space(value):
+    count = lax.axis_size("space")
+    nz = count // NXC
+    rows, cols = value.shape
+    return pl.pallas_call(
+        functools.partial(sum_kernel, nz),
+        out_shape=jax.ShapeDtypeStruct(value.shape, value.dtype),
+        in_specs=[pl.BlockSpec(memory_space=pltpu.VMEM)],
+        out_specs=pl.BlockSpec(memory_space=pltpu.VMEM),
+        scratch_shapes=[
+            pltpu.VMEM((NXC - 1, rows // NXC, cols), jnp.float32),
+            pltpu.VMEM((nz, rows // count, cols), jnp.float32),
+            pltpu.VMEM((nz - 1, rows // count, cols), jnp.float32),
+            pltpu.VMEM((nz, rows // count, cols), jnp.float32),
+            pltpu.SemaphoreType.DMA((4,)),
+            pltpu.SemaphoreType.DMA((4,)),
+        ],
+        compiler_params=pltpu.CompilerParams(collective_id=0, has_side_effects=True),
+    )(value)
 
 
 def padded_2(shard, sides, width):
@@ -101,7 +191,8 @@
         image = weighted(own_block)
         local_diag = gram_of(image, own_block)
         local_cross = gram_of(image, incoming)
-        own_diag, cross = lax.psum((local_diag, local_cross), "space")
+        total = sum_over_space(jnp.concatenate([local_diag, local_cross], axis=0))
+        own_diag, cross = total[:128], total[128:]
         peer_diag = from_partner(own_diag, "blk", sweep_round)
         keep_mat, take_mat = rotation(own_diag, peer_diag, cross, parity)
         own_block = mix_blocks(own_block, incoming, keep_mat, take_mat)

time: 1130 us -> 228 us (0.20); the launches traced: 1110 us -> 224 us
  waiting for transfers between devices: 961 us -> 22.7 us
  Pallas kernels: 0 us -> 87.2 us
  starting transfers between devices: 53.3 us -> 35.3 us
  between operations: 13.7 us -> 0.42 us
    psum x2 -> x0, waiting for transfers between devices: 939 us -> none  [shards(): own_diag, cross = lax.psum((local_diag, local_cross), 'space')]
    pallas_call x0 -> x2, Pallas kernels: none -> 87.2 us  [sum_over_space(): pl.pallas_call(functools.partial(sum_kernel, nz), out_shape=jax.ShapeDtyp...]
    ppermute x4, starting transfers between devices: 46.9 us -> 29.8 us  [from_partner(): return lax.ppermute(block, axis, route)]
  transfers between devices with their start and end apart: 10 -> 8, of which waited for: 8 -> 6; matrix products, arithmetic and copies ran while one was open for 2% -> 6% of each run, Pallas kernels for 0% -> 0%
where the time goes in v1:
time: 228 us; the launch traced here: 224 us
  Pallas kernels  87.2 us (38%)
  other arithmetic  52.3 us (23%)
  starting transfers between devices  35.3 us (15%)
  waiting for transfers between devices  22.7 us (10%)
  matrix products  16.2 us (7%)
  local copies, waits for them, and re-layouts  9.82 us (4%)
    pallas_call x2, Pallas kernels, sum_over_space(): pl.pallas_call(functools.partial(sum_kernel, nz), out_shape=jax.ShapeDtyp...  87.2 us
    ppermute x4, starting transfers between devices, from_partner(): return lax.ppermute(block, axis, route)  29.8 us
    another operation x6, other arithmetic, rotation(): factor = jnp.linalg.cholesky(normal_mat)  24.8 us
    another operation x4, other arithmetic, rotation(): inverse = jax.scipy.linalg.cho_solve((factor, True), eye_mat)  20.9 us
    ppermute x4, waiting for transfers between devices, from_partner(): return lax.ppermute(block, axis, route)  12 us
    ppermute x2, waiting for transfers between devices, padded_2(): after = lax.ppermute(first, axis, down)  8.5 us
    dot_general x4, matrix products, gram_of(): lax.dot_general(left.reshape(-1, width), right.reshape(-1, width), (((0,)...  7.49 us
    add x2, other arithmetic, weighted(): return block + (degree[..., None] * block - near)  5.04 us
  transfers between devices with their start and end apart: 8, of which 6 were waited for; matrix products, arithmetic and copies ran while one was open for 6% of the time, Pallas kernels for 0%

profile of v1, /device:TPU:1, one launch (start us, length us, event | category | flops | bytes accessed | tf_op | source)
XLA Modules:
  0.0 223.9 jit_solution(18444564273903169918)
XLA Ops:
  0.0 16.1 %collective-permute-start.2 = (f32[8,16,16,128]{3,2,1,0:T(8,128)}, f32[8,16,16,128]{3,2,1,0:T(8,128)S(1)}, u32[]{:S(2)}, u32[]{:S(2)}) collective-permute-start(f32[8,16,16,128]{3,2,1,0:T(8,128)} %param.4), channel_id=1, source_target_pairs={{0,1},{1,0},{2,3},{3,2},{4,5},{5,4},{6,7},{7,6},{8,9},{9,8},{10,11... | collective-permute-start | bytes 3145736 | tf_op jit(solution)/shard_map/ppermute | solution.py:119
  16.1 1.0 fusion.37
  17.1 1.3 collective-permute-start.1
  18.4 1.3 collective-permute-start
  19.9 1.6 collective-permute-done.1
  21.5 3.9 %collective-permute-done = f32[1,16,16,128]{3,2,1,0:T(8,128)S(1)} collective-permute-done((f32[1,16,16,128]{3,2,1,0:T(8,128)S(1)}, f32[1,16,16,128]{3,2,1,0:T(8,128)S(1)}, u32[]{:S(2)}, u32[]{:S(2)}) %collective-permute-start) | collective-permute-done | bytes 131104 | tf_op jit(solution)/shard_map/ppermute | solution.py:107
  25.4 4.6 %fusion.7 = f32[8,16,16,128]{3,2,1,0:T(8,128)S(1)} fusion(f32[8,16,16,128]{3,2,1,0:T(8,128)} %param.4, f32[1,16,16,128]{3,2,1,0:T(8,128)S(1)} %collective-permute-done.1, f32[1,16,16,128]{3,2,1,0:T(8,128)S(1)} %collective-permute-done, f32[8,16,16]{2,1,0:T(8,128)S(1)} %broadcast_add_fusion), kind=kLoop, calls=%fused_computation.30 | loop fusion | flops 2621440 | bytes 2367488 | tf_op jit(solution)/shard_map/add | solution.py:139
  30.0 1.9 convolution_bitcast_fusion.2
  31.9 1.9 convolution_bitcast_fusion.1
  33.8 0.7 pad_maximum_fusion.4.in_ref
  34.4 50.5 %shard_map.17 = f32[256,128]{1,0:T(8,128)} custom-call(f32[256,128]{1,0:T(8,128)} %pad_maximum_fusion.4.in_ref), custom_call_target="tpu_custom_call" | custom-call | tf_op jit(solution)/shard_map/pallas_call | solution.py:82
  84.9 0.9 slice.91
  85.8 7.3 %collective-permute-start.3 = (f32[128,128]{1,0:T(8,128)S(1)}, f32[128,128]{1,0:T(8,128)S(1)}, u32[]{:S(2)}, u32[]{:S(2)}) collective-permute-start(f32[128,128]{1,0:T(8,128)S(1)} %slice.91), channel_id=1, source_target_pairs={{0,1},{1,0},{2,3},{3,2},{4,5},{5,4},{6,7},{7,6},{8,9},{9,8},{10,11... | collective-permute-start | bytes 196616 | tf_op jit(solution)/shard_map/ppermute | solution.py:119
  93.2 1.2 gather_fusion
  94.4 1.2 gather_fusion.1
  95.7 0.3 convolution_add_fusion.3
  96.2 11.7 %cholesky.44 = f32[128,128]{1,0:T(8,128)S(1)} custom-call(f32[128,128]{1,0:T(8,128)S(1)} %fusion.33), custom_call_target="Cholesky" | custom-call | tf_op jit(solution)/shard_map/jit(cholesky)/cholesky | solution.py:160
  107.9 0.6 compare_reduce_fusion.1
  108.5 0.7 fusion.20
  109.2 9.8 %custom-call.18 = f32[1,128,128]{1,2,0:T(8,128)S(1)} custom-call(f32[1,128,128]{2,1,0:T(8,128)S(1)} %fusion.20), custom_call_target="InvertDiagBlocksLowerTriangular" | custom-call | tf_op jit(solution)/shard_map/jit(_cho_solve)/triangular_solve | solution.py:161
  119.9 1.0 fusion.38
  121.2 1.1 convolution_add_fusion.1
  122.3 0.3 copy.16
  122.6 3.2 %collective-permute-start.6 = (f32[8,16,16,128]{3,2,1,0:T(8,128)S(1)}, f32[8,16,16,128]{3,2,1,0:T(8,128)S(1)}, u32[]{:S(2)}, u32[]{:S(2)}) collective-permute-start(f32[8,16,16,128]{3,2,1,0:T(8,128)S(1)} %bitcast.80), channel_id=1, source_target_pairs={{0,2},{2,0},{1,3},{3,1},{4,6},{6,4},{5,7},{7,5},{8,10},{10,8},{9,1... | collective-permute-start | bytes 3145736 | tf_op jit(solution)/shard_map/ppermute | solution.py:119
  125.8 0.8 copy.18
  126.6 1.5 collective-permute-start.5
  128.1 0.7 copy.17
  128.8 1.5 collective-permute-start.4
  130.3 0.6 collective-permute-done.5
  131.0 4.6 %collective-permute-done.4 = f32[1,16,16,128]{3,2,1,0:T(8,128)S(1)} collective-permute-done((f32[1,16,16,128]{3,2,1,0:T(8,128)}, f32[1,16,16,128]{3,2,1,0:T(8,128)S(1)}, u32[]{:S(2)}, u32[]{:S(2)}) %collective-permute-start.4) | collective-permute-done | bytes 131104 | tf_op jit(solution)/shard_map/ppermute | solution.py:107
  135.5 0.4 fusion.13
  136.0 1.9 fusion.39
  137.9 11.4 %collective-permute-done.6 = f32[8,16,16,128]{3,2,1,0:T(8,128)S(1)} collective-permute-done((f32[8,16,16,128]{3,2,1,0:T(8,128)S(1)}, f32[8,16,16,128]{3,2,1,0:T(8,128)S(1)}, u32[]{:S(2)}, u32[]{:S(2)}) %collective-permute-start.6) | collective-permute-done | bytes 1048608 | tf_op jit(solution)/shard_map/ppermute | solution.py:119
  149.3 1.9 convolution_bitcast_fusion
  151.1 0.7 pad_maximum_fusion.5.in_ref
  151.8 36.7 %shard_map.18 = f32[256,128]{1,0:T(8,128)} custom-call(f32[256,128]{1,0:T(8,128)} %pad_maximum_fusion.5.in_ref), custom_call_target="tpu_custom_call" | custom-call | tf_op jit(solution)/shard_map/pallas_call | solution.py:82
  188.5 0.9 slice.103
  189.4 3.2 %collective-permute-start.7 = (f32[128,128]{1,0:T(8,128)S(1)}, f32[128,128]{1,0:T(8,128)S(1)}, u32[]{:S(2)}, u32[]{:S(2)}) collective-permute-start(f32[128,128]{1,0:T(8,128)S(1)} %slice.103), channel_id=1, source_target_pairs={{0,2},{2,0},{1,3},{3,1},{4,6},{6,4},{5,7},{7,5},{8,10},{10,8},{9,1... | collective-permute-start | bytes 196616 | tf_op jit(solution)/shard_map/ppermute | solution.py:119
  192.6 1.2 gather_fusion.2
  193.9 0.5 collective-permute-done.7
  194.4 1.2 gather_fusion.3
  195.7 0.3 convolution_add_fusion.2
  196.2 11.7 %cholesky.55 = f32[128,128]{1,0:T(8,128)S(1)} custom-call(f32[128,128]{1,0:T(8,128)S(1)} %fusion.27), custom_call_target="Cholesky" | custom-call | tf_op jit(solution)/shard_map/jit(cholesky)/cholesky | solution.py:160
  207.9 0.6 compare_reduce_fusion
  208.5 0.7 fusion.21
  209.2 9.8 %custom-call.20 = f32[1,128,128]{1,2,0:T(8,128)S(1)} custom-call(f32[1,128,128]{2,1,0:T(8,128)S(1)} %fusion.21), custom_call_target="InvertDiagBlocksLowerTriangular" | custom-call | tf_op jit(solution)/shard_map/jit(_cho_solve)/triangular_solve | solution.py:161
  219.9 1.8 fusion.40
  222.0 2.0 convolution_add_fusion
  (28 shorter events, 2.7 us)
Async XLA Ops:
  0.0 31.9 %collective-permute-start.2 = (f32[8,16,16,128]{3,2,1,0:T(8,128)}, f32[8,16,16,128]{3,2,1,0:T(8,128)S(1)}, u32[]{:S(2)}, u32[]{:S(2)}) collective-permute-start(f32[8,16,16,128]{3,2,1,0:T(8,128)} %param.4), channel_id=1, source_target_pairs={{0,1},{1,0},{2,3},{3,2},{4,5},{5,4},{6,7},{7,6},{8,9},{9,8},{10,11... | collective-permute-start | bytes 3145736 | tf_op jit(solution)/shard_map/ppermute | solution.py:119
  17.1 4.4 %collective-permute-start.1 = (f32[1,16,16,128]{3,2,1,0:T(8,128)S(1)}, f32[1,16,16,128]{3,2,1,0:T(8,128)S(1)}, u32[]{:S(2)}, u32[]{:S(2)}) collective-permute-start(f32[1,16,16,128]{3,2,1,0:T(8,128)S(1)} %get-tuple-element.10), channel_id=1, source_target_pairs={{0,8},{8,16},{16,24},{24,32},{32,40},{40,48},{48,56},{56,64},{64,7... | collective-permute-start | bytes 393224 | tf_op jit(solution)/shard_map/ppermute | solution.py:106
  18.4 7.0 %collective-permute-start = (f32[1,16,16,128]{3,2,1,0:T(8,128)S(1)}, f32[1,16,16,128]{3,2,1,0:T(8,128)S(1)}, u32[]{:S(2)}, u32[]{:S(2)}) collective-permute-start(f32[1,16,16,128]{3,2,1,0:T(8,128)S(1)} %get-tuple-element.9), channel_id=1, source_target_pairs={{8,0},{16,8},{24,16},{32,24},{40,32},{48,40},{56,48},{64,56},{72,6... | collective-permute-start | bytes 393224 | tf_op jit(solution)/shard_map/ppermute | solution.py:107
  19.9 10.1 %copy-start = (f32[8,16,16,128]{3,2,1,0:T(8,128)S(1)}, f32[8,16,16,128]{3,2,1,0:T(8,128)}, u32[]{:S(2)}) copy-start(f32[8,16,16,128]{3,2,1,0:T(8,128)} %param.4) | copy-start | bytes 3145732
  84.9 10.8 %copy-start.2 = (f32[256,128]{1,0:T(8,128)S(1)}, f32[256,128]{1,0:T(8,128)}, u32[]{:S(2)}) copy-start(f32[256,128]{1,0:T(8,128)} %shard_map.17) | copy-start | bytes 393220
  85.8 8.6 %collective-permute-start.3 = (f32[128,128]{1,0:T(8,128)S(1)}, f32[128,128]{1,0:T(8,128)S(1)}, u32[]{:S(2)}, u32[]{:S(2)}) collective-permute-start(f32[128,128]{1,0:T(8,128)S(1)} %slice.91), channel_id=1, source_target_pairs={{0,1},{1,0},{2,3},{3,2},{4,5},{5,4},{6,7},{7,6},{8,9},{9,8},{10,11... | collective-permute-start | bytes 196616 | tf_op jit(solution)/shard_map/ppermute | solution.py:119
  122.6 26.7 %collective-permute-start.6 = (f32[8,16,16,128]{3,2,1,0:T(8,128)S(1)}, f32[8,16,16,128]{3,2,1,0:T(8,128)S(1)}, u32[]{:S(2)}, u32[]{:S(2)}) collective-permute-start(f32[8,16,16,128]{3,2,1,0:T(8,128)S(1)} %bitcast.80), channel_id=1, source_target_pairs={{0,2},{2,0},{1,3},{3,1},{4,6},{6,4},{5,7},{7,5},{8,10},{10,8},{9,1... | collective-permute-start | bytes 3145736 | tf_op jit(solution)/shard_map/ppermute | solution.py:119
  126.6 4.4 %collective-permute-start.5 = (f32[1,16,16,128]{3,2,1,0:T(8,128)}, f32[1,16,16,128]{3,2,1,0:T(8,128)S(1)}, u32[]{:S(2)}, u32[]{:S(2)}) collective-permute-start(f32[1,16,16,128]{3,2,1,0:T(8,128)} %bitcast.85), channel_id=1, source_target_pairs={{0,8},{8,16},{16,24},{24,32},{32,40},{40,48},{48,56},{56,64},{64,7... | collective-permute-start | bytes 393224 | tf_op jit(solution)/shard_map/ppermute | solution.py:106
  128.8 6.7 %collective-permute-start.4 = (f32[1,16,16,128]{3,2,1,0:T(8,128)}, f32[1,16,16,128]{3,2,1,0:T(8,128)S(1)}, u32[]{:S(2)}, u32[]{:S(2)}) collective-permute-start(f32[1,16,16,128]{3,2,1,0:T(8,128)} %bitcast.86), channel_id=1, source_target_pairs={{8,0},{16,8},{24,16},{32,24},{40,32},{48,40},{56,48},{64,56},{72,6... | collective-permute-start | bytes 393224 | tf_op jit(solution)/shard_map/ppermute | solution.py:107
  188.5 7.2 %copy-start.1 = (f32[256,128]{1,0:T(8,128)S(1)}, f32[256,128]{1,0:T(8,128)}, u32[]{:S(2)}) copy-start(f32[256,128]{1,0:T(8,128)} %shard_map.18) | copy-start | bytes 393220
  189.4 5.0 %collective-permute-start.7 = (f32[128,128]{1,0:T(8,128)S(1)}, f32[128,128]{1,0:T(8,128)S(1)}, u32[]{:S(2)}, u32[]{:S(2)}) collective-permute-start(f32[128,128]{1,0:T(8,128)S(1)} %slice.103), channel_id=1, source_target_pairs={{0,2},{2,0},{1,3},{3,1},{4,6},{6,4},{5,7},{7,5},{8,10},{10,8},{9,1... | collective-permute-start | bytes 196616 | tf_op jit(solution)/shard_map/ppermute | solution.py:119

commit v2 on v0

v2 whole, which is shorter than its diff:
```python
import functools

import jax
import jax.numpy as jnp
from jax import lax
from jax.experimental import pallas as pl
from jax.experimental.pallas import tpu as pltpu
from jax.sharding import PartitionSpec as P

NXC = 4
GROUP = 4
BOX = 4
WIDTH = 128
F32, BF16 = jnp.float32, jnp.bfloat16
MESH = pl.DeviceIdType.MESH
ROWS_IN, ROWS_OUT = (((0,), (0,)), ((), ())), (((1,), (0,)), ((), ()))
LANES = (((1,), (1,)), ((), ()))
Z_IN = (-2, -1, 1)
Z_OUT = (-1, 1, 2)


def halves(value):
    high = value.astype(BF16)
    return high, (value - high.astype(F32)).astype(BF16)


def dot3(left, right, dims=ROWS_OUT):
    (lh, ll), (rh, rl) = left, right

    def dot(u, v):
        return lax.dot_general(u, v, dims, preferred_element_type=F32)

    return dot(lh, rh) + (dot(lh, rl) + dot(ll, rh))


def mul(left, right, dims=ROWS_OUT):
    return dot3(halves(left), halves(right), dims)


def eye_mask():
    shape = (WIDTH, WIDTH)
    return lax.broadcasted_iota(jnp.int32, shape, 0) == lax.broadcasted_iota(jnp.int32, shape, 1)


def inverse_of(matrix):
    panels = [matrix[8 * i : 8 * i + 8] for i in range(WIDTH // 8)]
    lane = lax.broadcasted_iota(jnp.int32, (8, WIDTH), 1)
    sub = lax.broadcasted_iota(jnp.int32, (8, WIDTH), 0)
    for k in range(WIDTH):
        home, s = k // 8, k % 8
        row = panels[home][s : s + 1]
        pivot = 1.0 / row[:, k : k + 1]
        row = jnp.where(lane[:1] == k, pivot, row * pivot)
        for i in range(len(panels)):
            old = panels[i]
            new = jnp.where(lane == k, 0.0, old) - old[:, k : k + 1] * row
            if i == home:
                new = jnp.where(sub == s, row, new)
            panels[i] = new
    return jnp.concatenate(panels, axis=0)


def rotation(own_col, peer_row, cross, parity):
    eye = jnp.where(eye_mask(), 1.0, 0.0)
    ratios = cross / (own_col + peer_row)
    inverse = inverse_of(eye + mul(ratios, ratios, LANES))
    solved = mul(inverse, ratios)
    return 2.0 * inverse - eye, (2.0 * parity) * solved.T


def kernel(nz, x_ref, out_ref, xp, xq, xq1, halo, w, wp, out_half, in_half, xh, xl, xph, xpl, wh, wl, first_h, first_l, bufs_a, bufs_b, core_a, keep_give, kt, ktq, send, recv):
    space, blk = lax.axis_index("space"), lax.axis_index("blk")
    count = nz * NXC
    z, x = space // NXC, space % NXC
    b4 = blk % GROUP
    base, low, high = blk - b4, b4 % 2, b4 // 2
    core = (space, base + 2 * high + 1 - low)
    peer_y = (space, base + (b4 + 2) % GROUP)
    after = ((space + 1) % count, blk)
    before = ((space + count - 1) % count, blk)
    layers = x_ref.shape[0]
    half = layers // 2

    def at(dz=0, dx=0, block=None):
        return (((z + dz + nz) % nz) * NXC + (x + dx) % NXC, blk if block is None else block)

    group = [at(0, g // GROUP, base + (b4 + g % GROUP) % GROUP) for g in range(1, NXC * GROUP)]
    rings = [at(dz) for dz in (-BOX, -2, -1, 1, 2, BOX)]

    copies = []

    def push(src, dst, device):
        index = len(copies)
        copy = pltpu.make_async_remote_copy(
            src_ref=src,
            dst_ref=dst,
            send_sem=send.at[index],
            recv_sem=recv.at[index],
            device_id=device,
            device_id_type=MESH,
        )
        copy.start()
        copies.append(copy)
        return copy

    def landed(*some):
        for copy in some:
            copy.wait_recv()

    barrier = pltpu.get_barrier_semaphore()
    peers = group + rings + [after, before]
    for device in peers:
        pl.semaphore_signal(barrier, inc=1, device_id=device, device_id_type=MESH)
    there, here = (1 - high) * half, high * half
    rows = x_ref.shape[1]
    side = rows // 16
    row = lax.broadcasted_iota(jnp.int32, (rows, WIDTH), 0)
    pos_y, pos_z = row // 16, row % 16

    def flag(cond):
        return jnp.where(cond, 1.0, 0.0)

    lowest, highest = flag(space > 0), flag(space < count - 1)
    plane = flag(pos_y > 0) + flag(pos_y < side - 1) + flag(pos_z > 0) + flag(pos_z < 15)
    zero16 = jnp.zeros((16, WIDTH), F32)

    def image(i, up, down, deg_x):
        cur = x_ref[i]
        near = up + down
        near = near + jnp.concatenate([cur[16:], zero16], axis=0)
        near = near + jnp.concatenate([zero16, cur[:-16]], axis=0)
        near = near + jnp.where(pos_z < 15, pltpu.roll(cur, rows - 1, 0), 0.0)
        near = near + jnp.where(pos_z > 0, pltpu.roll(cur, 1, 0), 0.0)
        value = cur + ((plane + deg_x) * cur - near)
        w[i] = value
        wh[i], wl[i] = halves(value)

    @pl.loop(1, layers - 1)
    def _(i):
        image(i, x_ref[i + 1], x_ref[i - 1], 2.0)

    def chunk(c):
        out_half[c] = jnp.where(high == 0, w[there + c], x_ref[there + c])
        return push(out_half.at[c], in_half.at[c], peer_y)

    pl.semaphore_wait(barrier, len(peers))
    chunks = [chunk(c) for c in range(half - 1)]
    halos = [push(x_ref.at[layers - 1], halo.at[0], after), push(x_ref.at[0], halo.at[1], before)]
    whole = push(x_ref, xp, core)

    @pl.loop(0, layers)
    def _(i):
        xh[i], xl[i] = halves(x_ref[i])

    landed(*halos)
    image(0, x_ref[1], jnp.where(space > 0, halo[0], 0.0), 1.0 + lowest)
    image(layers - 1, jnp.where(space < count - 1, halo[1], 0.0), x_ref[layers - 2], 1.0 + highest)
    chunks.append(chunk(half - 1))
    images = push(w.at[pl.ds(here, half)], wp, core)

    landed(whole)

    def gram_own(i, total):
        ph, plow = halves(xp[i])
        xph[i], xpl[i] = ph, plow
        right = (jnp.concatenate([xh[i], ph], axis=1), jnp.concatenate([xl[i], plow], axis=1))
        return total + dot3((wh[i], wl[i]), right, ROWS_IN)

    gram = lax.fori_loop(0, layers, gram_own, jnp.zeros((WIDTH, 2 * WIDTH), F32))
    ga, rxa, sa, rza, ringa, ta, gza, fa = bufs_a
    gb, rxb, sb, rzb, ringb, tb, gzb, fb = bufs_b
    for t in range(WIDTH // 8):
        ga[t // BOX, t % BOX, 0] = gram[8 * t : 8 * t + 8, :WIDTH]
        ga[t // BOX, t % BOX, 1] = gram[8 * t : 8 * t + 8, WIDTH:]

    def over_x(src, dst):
        return [push(src.at[(x + d) % NXC], dst.at[d - 1], at(0, d)) for d in range(1, NXC)]

    def over_z(src, dst):
        return [push(src.at[(z + o + nz) % BOX], dst.at[j], at(o)) for j, o in enumerate(Z_IN)]

    def ring_step(k, own, slots, boxes):
        up = boxes // 2
        out = [push(own if k == 0 else slots.at[k - 1], slots.at[k], at(BOX))]
        if k < boxes - 1 - up:
            out.append(push(own if k == 0 else slots.at[up + k - 1], slots.at[up + k], at(-BOX)))
        return out

    def back_z(src, dst):
        return [push(src, dst.at[z % BOX], at(o)) for o in Z_OUT]

    boxes = nz // BOX

    a_x = over_x(ga, rxa)
    landed(images)
    cross_own = jnp.zeros((WIDTH, WIDTH), F32)
    cross_peer = jnp.zeros((WIDTH, WIDTH), F32)
    a_z = None
    for c in range(half):
        landed(chunks[c])
        right = halves(in_half[c])
        own_left = halves(jnp.where(high == 0, w[here + c], x_ref[here + c]))
        peer_left = halves(jnp.where(high == 0, wp[c], xp[here + c]))
        cross_own = cross_own + dot3(own_left, right, ROWS_IN)
        cross_peer = cross_peer + dot3(peer_left, right, ROWS_IN)
        if c == half // 2 - 1:
            landed(*a_x)
            sa[...] = ga[x] + rxa[0] + rxa[1] + rxa[2]
            a_z = over_z(sa, rza)
    keep = jnp.where(high == 0, cross_own, cross_peer.T)
    give = jnp.where(high == 0, cross_peer, cross_own.T)
    for t in range(WIDTH // 8):
        gb[t // BOX, t % BOX] = keep[8 * t : 8 * t + 8]
        keep_give[t // BOX, t % BOX] = give[8 * t : 8 * t + 8]
    owner = base + (1 - high) * (3 - b4) + high * (b4 - 2)
    b_x = over_x(gb, rxb)
    b_x += [push(keep_give.at[(x + d) % NXC], rxb.at[3 + d], at(0, d, owner)) for d in range(NXC)]
    rest = push(x_ref, xq, peer_y)

    landed(*a_z)
    ta[...] = sa[z % BOX] + rza[0] + rza[1] + rza[2]
    a_r = ring_step(0, ta, ringa, boxes)
    landed(*b_x)
    total = gb[x]
    for j in range(7):
        total = total + rxb[j]
    sb[...] = total
    b_z = over_z(sb, rzb)
    steps = boxes // 2
    landed(*a_r)
    a_r = ring_step(1, ta, ringa, boxes)
    landed(*b_z)
    tb[...] = sb[z % BOX] + rzb[0] + rzb[1] + rzb[2]
    b_r = ring_step(0, tb, ringb, boxes)
    for k in range(2, steps):
        landed(*a_r)
        a_r = ring_step(k, ta, ringa, boxes)
        landed(*b_r)
        b_r = ring_step(k - 1, tb, ringb, boxes)
    landed(*a_r)
    total = ta[...]
    for j in range(boxes - 1):
        total = total + ringa[j]
    gza[z % BOX] = total
    a_g = back_z(gza.at[z % BOX], gza)
    landed(*b_r)
    b_r = ring_step(steps - 1, tb, ringb, boxes)
    landed(*a_g)
    fa[x] = gza[...]
    a_g = [push(fa.at[x], fa.at[x], at(0, d)) for d in range(1, NXC)]
    landed(*b_r)
    total = tb[...]
    for j in range(boxes - 1):
        total = total + ringb[j]
    gzb[z % BOX] = total
    b_g = back_z(gzb.at[z % BOX], gzb)
    landed(*a_g)
    a_c = push(fa, core_a, core)
    landed(*b_g)
    fb[b4, x] = gzb[...]
    b_g = [push(fb.at[b4, x], fb.at[b4, x], device) for device in group]

    landed(rest)
    forward = push(xq, xq1, core)
    landed(a_c)
    square = (WIDTH, WIDTH)
    own_a, own_c = fa[:, :, 0].reshape(square), fa[:, :, 1].reshape(square)
    peer_a, peer_c = core_a[:, :, 0].reshape(square), core_a[:, :, 1].reshape(square)
    eye = eye_mask()

    def column(values):
        return jnp.sum(jnp.where(eye, values, 0.0), axis=1, keepdims=True)

    def diag_row(values):
        return jnp.sum(jnp.where(eye, values, 0.0), axis=0, keepdims=True)

    keep_m, take_m = rotation(column(own_a), diag_row(peer_a), own_c, jnp.where(low == 1, 1.0, -1.0))
    pair = jnp.concatenate([keep_m, take_m], axis=0)
    full = jnp.concatenate(
        [jnp.concatenate([own_a, own_c], axis=1), jnp.concatenate([peer_c, peer_a], axis=1)], axis=0
    )
    own_diag = jnp.sum(pair * mul(full, pair), axis=0, keepdims=True)
    kt[: 2 * WIDTH] = pair
    kt[2 * WIDTH :] = jnp.broadcast_to(own_diag, (8, WIDTH))
    turn = push(kt, ktq, peer_y)

    def wide(pair):
        ph, plow = halves(pair)
        return jnp.concatenate([ph, plow], axis=1), ph

    def mixed(lh, ll, right):
        both, ph = right
        part = lax.dot_general(lh, both, ROWS_OUT, preferred_element_type=F32)
        last = lax.dot_general(ll, ph, ROWS_OUT, preferred_element_type=F32)
        return part[:, :WIDTH] + (part[:, WIDTH:] + last)

    own_wide = wide(pair)

    @pl.loop(0, layers)
    def _(i):
        lh = jnp.concatenate([xh[i], xph[i]], axis=1)
        ll = jnp.concatenate([xl[i], xpl[i]], axis=1)
        first_h[i, :, :WIDTH], first_l[i, :, :WIDTH] = halves(mixed(lh, ll, own_wide))

    landed(forward, turn)
    pair_q = ktq[: 2 * WIDTH]
    diag_q = ktq[2 * WIDTH : 2 * WIDTH + 1]
    peer_wide = wide(pair_q)

    @pl.loop(0, layers)
    def _(i):
        qh, ql = halves(xq[i])
        q1h, q1l = halves(xq1[i])
        lh, ll = jnp.concatenate([qh, q1h], axis=1), jnp.concatenate([ql, q1l], axis=1)
        first_h[i, :, WIDTH:], first_l[i, :, WIDTH:] = halves(mixed(lh, ll, peer_wide))

    landed(*b_g)
    top = jnp.concatenate([fb[low].reshape(square), fb[2 + low].reshape(square)], axis=1)
    bottom = jnp.concatenate([fb[3 - low].reshape(square), fb[1 - low].reshape(square)], axis=1)
    cross = jnp.concatenate([top, bottom], axis=0)
    left = jnp.where(high == 0, pair, pair_q)
    right = jnp.where(high == 0, pair_q, pair)
    turned = mul(left, mul(cross, right), ROWS_IN)
    turned = jnp.where(high == 0, turned, turned.T)
    keep_m, take_m = rotation(column(own_diag), diag_q, turned, jnp.where(high == 1, 1.0, -1.0))
    last_wide = wide(jnp.concatenate([keep_m, take_m], axis=0))

    @pl.loop(0, layers)
    def _(i):
        out_ref[i] = mixed(first_h[i], first_l[i], last_wide)

    for copy in copies:
        copy.wait_send()


def rotate(block):
    nz = lax.axis_size("space") // NXC
    layers, rows, _ = block.shape
    half = layers // 2
    boxes = nz // BOX
    full = pltpu.VMEM((layers, rows, WIDTH), F32)
    part = pltpu.VMEM((layers, rows, WIDTH), BF16)
    double = pltpu.VMEM((layers, rows, 2 * WIDTH), BF16)

    def sums(arrivals, trail, blocks):
        return [
            pltpu.VMEM((NXC, BOX) + trail, F32),
            pltpu.VMEM((arrivals, BOX) + trail, F32),
            pltpu.VMEM((BOX,) + trail, F32),
            pltpu.VMEM((3,) + trail, F32),
            pltpu.VMEM((boxes - 1,) + trail, F32),
            pltpu.VMEM(trail, F32),
            pltpu.VMEM((BOX,) + trail, F32),
            pltpu.VMEM(blocks + (NXC, BOX) + trail, F32),
        ]

    trail_a, trail_b = (2, 8, WIDTH), (8, WIDTH)
    return pl.pallas_call(
        functools.partial(kernel, nz),
        out_shape=jax.ShapeDtypeStruct(block.shape, F32),
        in_specs=[pl.BlockSpec(memory_space=pltpu.VMEM)],
        out_specs=pl.BlockSpec(memory_space=pltpu.VMEM),
        scratch_shapes=[
            full,
            full,
            full,
            pltpu.VMEM((2, rows, WIDTH), F32),
            full,
            pltpu.VMEM((half, rows, WIDTH), F32),
            pltpu.VMEM((half, rows, WIDTH), F32),
            pltpu.VMEM((half, rows, WIDTH), F32),
            part,
            part,
            part,
            part,
            part,
            part,
            double,
            double,
            sums(3, trail_a, ()),
            sums(7, trail_b, (GROUP,)),
            pltpu.VMEM((NXC, BOX) + trail_a, F32),
            pltpu.VMEM((NXC, BOX) + trail_b, F32),
            pltpu.VMEM((2 * WIDTH + 8, WIDTH), F32),
            pltpu.VMEM((2 * WIDTH + 8, WIDTH), F32),
            pltpu.SemaphoreType.DMA((80,)),
            pltpu.SemaphoreType.DMA((80,)),
        ],
        compiler_params=pltpu.CompilerParams(
            collective_id=0, has_side_effects=True, vmem_limit_bytes=48 * 1024 * 1024
        ),
    )(block)


def shards(snapshots):
    layers, cells_y, cells_z, width = snapshots.shape
    return rotate(snapshots.reshape(layers, cells_y * cells_z, width)).reshape(snapshots.shape)


def solution(mesh):
    return jax.shard_map(
        shards,
        mesh=mesh,
        in_specs=(P("space", None, None, "blk"),),
        out_specs=P("space", None, None, "blk"),
        check_vma=False,
    )
```

time: 1130 us -> 103 us (0.09); the launches traced: 1110 us -> 103 us
  waiting for transfers between devices: 961 us -> 0 us
  Pallas kernels: 0 us -> 101 us
  starting transfers between devices: 53.3 us -> 0 us
  other arithmetic: 51.7 us -> 0 us
  matrix products: 18.7 us -> 0 us
  between operations: 13.7 us -> 0.01 us
    psum x2 -> x0, waiting for transfers between devices: 939 us -> none  [shards(): own_diag, cross = lax.psum((local_diag, local_cross), 'space')]
    pallas_call x0 -> x1, Pallas kernels: none -> 101 us  [rotate(): pl.pallas_call(functools.partial(kernel, nz), out_shape=jax.ShapeDtypeStr...]
    ppermute x8 -> x0, starting transfers between devices: 53.2 us -> none  [the longest x4 46.9 us: from_partner(): return lax.ppermute(block, axis, route)]
    another operation x10 -> x0, other arithmetic: 45.7 us -> none  [the longest x6 24.8 us: rotation(): factor = jnp.linalg.cholesky(normal_mat)]
    ppermute x8 -> x0, waiting for transfers between devices: 21.4 us -> none  [the longest x4 10.8 us: from_partner(): return lax.ppermute(block, axis, route)]
    dot_general x10 -> x0, matrix products: 16.5 us -> none  [the longest x4 10 us: gram_of(): lax.dot_general(left.reshape(-1, width), right.reshape(-1, width), (((0,)...]
  transfers between devices with their start and end apart: 10 -> 0, of which waited for: 8 -> 0; matrix products, arithmetic and copies ran while one was open for 2% -> 0% of each run, Pallas kernels for 0% -> 0%
where the time goes in v2:
time: 103 us
  Pallas kernels  101 us (98%)
  local copies, waits for them, and re-layouts  2.2 us (2%)
    pallas_call x1, Pallas kernels, rotate(): pl.pallas_call(functools.partial(kernel, nz), out_shape=jax.ShapeDtypeStr...  101 us
    unnamed x3, local copies, waits for them, and re-layouts  2.2 us

profile of v2, /device:TPU:1, one launch (start us, length us, event | category | flops | bytes accessed | tf_op | source)
XLA Modules:
  0.0 103.0 jit_solution(10863091405557638093)
XLA Ops:
  0.0 0.0 copy-start
  0.0 1.2 %copy-done = f32[8,16,16,128]{3,2,1,0:T(8,128)S(1)} copy-done((f32[8,16,16,128]{3,2,1,0:T(8,128)S(1)}, f32[8,16,16,128]{3,2,1,0:T(8,128)}, u32[]{:S(2)}) %copy-start) | copy-done | bytes 1048600
  1.2 100.8 %shard_map.17 = f32[8,256,128]{2,1,0:T(8,128)S(1)} custom-call(f32[8,256,128]{2,1,0:T(8,128)S(1)} %bitcast.3), custom_call_target="tpu_custom_call" | custom-call | tf_op jit(solution)/shard_map/pallas_call | solution.py:358
  102.0 1.0 copy.3
Async XLA Ops:
  0.0 1.2 %copy-start = (f32[8,16,16,128]{3,2,1,0:T(8,128)S(1)}, f32[8,16,16,128]{3,2,1,0:T(8,128)}, u32[]{:S(2)}) copy-start(f32[8,16,16,128]{3,2,1,0:T(8,128)} %param.1) | copy-start | bytes 3145732

commit v3 on v2

--- a/solution.py
+++ b/solution.py
@@ -42,28 +42,52 @@
     return lax.broadcasted_iota(jnp.int32, shape, 0) == lax.broadcasted_iota(jnp.int32, shape, 1)
 
 
-def inverse_of(matrix):
-    panels = [matrix[8 * i : 8 * i + 8] for i in range(WIDTH // 8)]
-    lane = lax.broadcasted_iota(jnp.int32, (8, WIDTH), 1)
-    sub = lax.broadcasted_iota(jnp.int32, (8, WIDTH), 0)
-    for k in range(WIDTH):
-        home, s = k // 8, k % 8
-        row = panels[home][s : s + 1]
-        pivot = 1.0 / row[:, k : k + 1]
-        row = jnp.where(lane[:1] == k, pivot, row * pivot)
-        for i in range(len(panels)):
+def inverse_of(matrix, between):
+    count = WIDTH // 8
+    shape = (8, WIDTH)
+    panels = [matrix[8 * i : 8 * i + 8] for i in range(count)]
+    lane = lax.broadcasted_iota(jnp.int32, shape, 1)
+    sub = lax.broadcasted_iota(jnp.int32, shape, 0)
+    for home in range(count):
+        first = 8 * home
+        rows = [jnp.broadcast_to(panels[home][t : t + 1], shape) for t in range(8)]
+        entry = [[None] * 8 for _ in range(8)]
+        for t in range(8):
+            for u in range(t, 8):
+                place = rows[t][:, first + u : first + u + 1]
+                entry[t][u] = entry[u][t] = jnp.broadcast_to(place, shape)
+        block = (lane >= first) & (lane < first + 8)
+        for t in range(8):
+            rows[t] = jnp.where(block, jnp.where(lane == first + t, 1.0, 0.0), rows[t])
+        for t in range(8):
+            pivot = 1.0 / entry[t][t]
+            rows[t] = rows[t] * pivot
+            for v in range(t + 1, 8):
+                entry[t][v] = entry[t][v] * pivot
+            for u in range(8):
+                if u != t:
+                    rows[u] = rows[u] - entry[u][t] * rows[t]
+                    for v in range(t + 1, 8):
+                        entry[u][v] = entry[u][v] - entry[u][t] * entry[t][v]
+        for i in range(count):
             old = panels[i]
-            new = jnp.where(lane == k, 0.0, old) - old[:, k : k + 1] * row
             if i == home:
-                new = jnp.where(sub == s, row, new)
+                new = rows[0]
+                for t in range(1, 8):
+                    new = jnp.where(sub == t, rows[t], new)
+            else:
+                new = jnp.where(block, 0.0, old)
+                for t in range(8):
+                    new = new - old[:, first + t : first + t + 1] * rows[t]
             panels[i] = new
+        between(home)
     return jnp.concatenate(panels, axis=0)
 
 
-def rotation(own_col, peer_row, cross, parity):
+def rotation(own_col, peer_row, cross, parity, between):
     eye = jnp.where(eye_mask(), 1.0, 0.0)
     ratios = cross / (own_col + peer_row)
-    inverse = inverse_of(eye + mul(ratios, ratios, LANES))
+    inverse = inverse_of(eye + mul(ratios, ratios, LANES), between)
     solved = mul(inverse, ratios)
     return 2.0 * inverse - eye, (2.0 * parity) * solved.T
 
@@ -196,6 +220,7 @@
     cross_own = jnp.zeros((WIDTH, WIDTH), F32)
     cross_peer = jnp.zeros((WIDTH, WIDTH), F32)
     a_z = None
+    a_r = None
     for c in range(half):
         landed(chunks[c])
         right = halves(in_half[c])
@@ -203,10 +228,14 @@
         peer_left = halves(jnp.where(high == 0, wp[c], xp[here + c]))
         cross_own = cross_own + dot3(own_left, right, ROWS_IN)
         cross_peer = cross_peer + dot3(peer_left, right, ROWS_IN)
-        if c == half // 2 - 1:
+        if c == 0:
             landed(*a_x)
             sa[...] = ga[x] + rxa[0] + rxa[1] + rxa[2]
             a_z = over_z(sa, rza)
+        if c == half - 2:
+            landed(*a_z)
+            ta[...] = sa[z % BOX] + rza[0] + rza[1] + rza[2]
+            a_r = ring_step(0, ta, ringa, boxes)
     keep = jnp.where(high == 0, cross_own, cross_peer.T)
     give = jnp.where(high == 0, cross_peer, cross_own.T)
     for t in range(WIDTH // 8):
@@ -217,26 +246,24 @@
     b_x += [push(keep_give.at[(x + d) % NXC], rxb.at[3 + d], at(0, d, owner)) for d in range(NXC)]
     rest = push(x_ref, xq, peer_y)
 
-    landed(*a_z)
-    ta[...] = sa[z % BOX] + rza[0] + rza[1] + rza[2]
-    a_r = ring_step(0, ta, ringa, boxes)
+    steps = boxes // 2
+    landed(*a_r)
+    a_r = ring_step(1, ta, ringa, boxes)
     landed(*b_x)
     total = gb[x]
     for j in range(7):
         total = total + rxb[j]
     sb[...] = total
     b_z = over_z(sb, rzb)
-    steps = boxes // 2
     landed(*a_r)
-    a_r = ring_step(1, ta, ringa, boxes)
+    a_r = ring_step(2, ta, ringa, boxes)
     landed(*b_z)
     tb[...] = sb[z % BOX] + rzb[0] + rzb[1] + rzb[2]
     b_r = ring_step(0, tb, ringb, boxes)
-    for k in range(2, steps):
-        landed(*a_r)
-        a_r = ring_step(k, ta, ringa, boxes)
-        landed(*b_r)
-        b_r = ring_step(k - 1, tb, ringb, boxes)
+    landed(*a_r)
+    a_r = ring_step(3, ta, ringa, boxes)
+    landed(*b_r)
+    b_r = ring_step(1, tb, ringb, boxes)
     landed(*a_r)
     total = ta[...]
     for j in range(boxes - 1):
@@ -244,24 +271,20 @@
     gza[z % BOX] = total
     a_g = back_z(gza.at[z % BOX], gza)
     landed(*b_r)
-    b_r = ring_step(steps - 1, tb, ringb, boxes)
+    b_r = ring_step(2, tb, ringb, boxes)
     landed(*a_g)
     fa[x] = gza[...]
     a_g = [push(fa.at[x], fa.at[x], at(0, d)) for d in range(1, NXC)]
+    landed(*b_r)
+    b_r = ring_step(3, tb, ringb, boxes)
+    landed(*a_g)
+    a_c = push(fa, core_a, core)
     landed(*b_r)
     total = tb[...]
     for j in range(boxes - 1):
         total = total + ringb[j]
     gzb[z % BOX] = total
     b_g = back_z(gzb.at[z % BOX], gzb)
-    landed(*a_g)
-    a_c = push(fa, core_a, core)
-    landed(*b_g)
-    fb[b4, x] = gzb[...]
-    b_g = [push(fb.at[b4, x], fb.at[b4, x], device) for device in group]
-
-    landed(rest)
-    forward = push(xq, xq1, core)
     landed(a_c)
     square = (WIDTH, WIDTH)
     own_a, own_c = fa[:, :, 0].reshape(square), fa[:, :, 1].reshape(square)
@@ -274,7 +297,19 @@
     def diag_row(values):
         return jnp.sum(jnp.where(eye, values, 0.0), axis=0, keepdims=True)
 
-    keep_m, take_m = rotation(column(own_a), diag_row(peer_a), own_c, jnp.where(low == 1, 1.0, -1.0))
+    spread, moved = [], []
+
+    def serve(step):
+        if step == 6:
+            landed(*b_g)
+            fb[b4, x] = gzb[...]
+            spread.extend(push(fb.at[b4, x], fb.at[b4, x], device) for device in group)
+        if step == 11:
+            landed(rest)
+            moved.append(push(xq, xq1, core))
+
+    sign = jnp.where(low == 1, 1.0, -1.0)
+    keep_m, take_m = rotation(column(own_a), diag_row(peer_a), own_c, sign, serve)
     pair = jnp.concatenate([keep_m, take_m], axis=0)
     full = jnp.concatenate(
         [jnp.concatenate([own_a, own_c], axis=1), jnp.concatenate([peer_c, peer_a], axis=1)], axis=0
@@ -295,26 +330,11 @@
         return part[:, :WIDTH] + (part[:, WIDTH:] + last)
 
     own_wide = wide(pair)
-
-    @pl.loop(0, layers)
-    def _(i):
-        lh = jnp.concatenate([xh[i], xph[i]], axis=1)
-        ll = jnp.concatenate([xl[i], xpl[i]], axis=1)
-        first_h[i, :, :WIDTH], first_l[i, :, :WIDTH] = halves(mixed(lh, ll, own_wide))
-
-    landed(forward, turn)
+    landed(turn)
     pair_q = ktq[: 2 * WIDTH]
     diag_q = ktq[2 * WIDTH : 2 * WIDTH + 1]
     peer_wide = wide(pair_q)
-
-    @pl.loop(0, layers)
-    def _(i):
-        qh, ql = halves(xq[i])
-        q1h, q1l = halves(xq1[i])
-        lh, ll = jnp.concatenate([qh, q1h], axis=1), jnp.concatenate([ql, q1l], axis=1)
-        first_h[i, :, WIDTH:], first_l[i, :, WIDTH:] = halves(mixed(lh, ll, peer_wide))
-
-    landed(*b_g)
+    landed(*spread)
     top = jnp.concatenate([fb[low].reshape(square), fb[2 + low].reshape(square)], axis=1)
     bottom = jnp.concatenate([fb[3 - low].reshape(square), fb[1 - low].reshape(square)], axis=1)
     cross = jnp.concatenate([top, bottom], axis=0)
@@ -322,7 +342,22 @@
     right = jnp.where(high == 0, pair_q, pair)
     turned = mul(left, mul(cross, right), ROWS_IN)
     turned = jnp.where(high == 0, turned, turned.T)
-    keep_m, take_m = rotation(column(own_diag), diag_q, turned, jnp.where(high == 1, 1.0, -1.0))
+    landed(*moved)
+
+    def first_round(step):
+        i = step // 2
+        if step % 2 == 0:
+            lh = jnp.concatenate([xh[i], xph[i]], axis=1)
+            ll = jnp.concatenate([xl[i], xpl[i]], axis=1)
+            first_h[i, :, :WIDTH], first_l[i, :, :WIDTH] = halves(mixed(lh, ll, own_wide))
+        else:
+            qh, ql = halves(xq[i])
+            q1h, q1l = halves(xq1[i])
+            lh, ll = jnp.concatenate([qh, q1h], axis=1), jnp.concatenate([ql, q1l], axis=1)
+            first_h[i, :, WIDTH:], first_l[i, :, WIDTH:] = halves(mixed(lh, ll, peer_wide))
+
+    sign = jnp.where(high == 1, 1.0, -1.0)
+    keep_m, take_m = rotation(column(own_diag), diag_q, turned, sign, first_round)
     last_wide = wide(jnp.concatenate([keep_m, take_m], axis=0))
 
     @pl.loop(0, layers)

time: 103 us -> 91.1 us (0.88)
  Pallas kernels: 101 us -> 88.7 us
    pallas_call x1, Pallas kernels: 101 us -> 88.7 us  [rotate(): pl.pallas_call(functools.partial(kernel, nz), out_shape=jax.ShapeDtypeStr...]
where the time goes in v3:
time: 91.1 us; the launch traced here: 91 us
  Pallas kernels  88.7 us (97%)
  local copies, waits for them, and re-layouts  2.2 us (2%)
    pallas_call x1, Pallas kernels, rotate(): pl.pallas_call(functools.partial(kernel, nz), out_shape=jax.ShapeDtypeStr...  88.7 us
    unnamed x3, local copies, waits for them, and re-layouts  2.2 us

profile of v3, /device:TPU:1, one launch (start us, length us, event | category | flops | bytes accessed | tf_op | source)
XLA Modules:
  0.0 91.0 jit_solution(12152650313566090873)
XLA Ops:
  0.0 0.0 copy-start
  0.0 1.2 %copy-done = f32[8,16,16,128]{3,2,1,0:T(8,128)S(1)} copy-done((f32[8,16,16,128]{3,2,1,0:T(8,128)S(1)}, f32[8,16,16,128]{3,2,1,0:T(8,128)}, u32[]{:S(2)}) %copy-start) | copy-done | bytes 1048600
  1.2 88.7 %shard_map.17 = f32[8,256,128]{2,1,0:T(8,128)S(1)} custom-call(f32[8,256,128]{2,1,0:T(8,128)S(1)} %bitcast.3), custom_call_target="tpu_custom_call" | custom-call | tf_op jit(solution)/shard_map/pallas_call | solution.py:393
  90.0 1.0 %copy.3 = f32[8,16,16,128]{3,2,1,0:T(8,128)} copy(f32[8,16,16,128]{3,2,1,0:T(8,128)S(1)} %bitcast.2) | data formatting | bytes 2097152
Async XLA Ops:
  0.0 1.2 %copy-start = (f32[8,16,16,128]{3,2,1,0:T(8,128)S(1)}, f32[8,16,16,128]{3,2,1,0:T(8,128)}, u32[]{:S(2)}) copy-start(f32[8,16,16,128]{3,2,1,0:T(8,128)} %param.1) | copy-start | bytes 3145732

commit v4 on v3

--- a/solution.py
+++ b/solution.py
@@ -92,7 +92,7 @@
     return 2.0 * inverse - eye, (2.0 * parity) * solved.T
 
 
-def kernel(nz, x_ref, out_ref, xp, xq, xq1, halo, w, wp, out_half, in_half, xh, xl, xph, xpl, wh, wl, first_h, first_l, bufs_a, bufs_b, core_a, keep_give, kt, ktq, send, recv):
+def kernel(nz, x_ref, out_ref, xp, xq, xq1, halo, w, wp, out_half, in_half, xh, xl, xph, xpl, wh, wl, first_h, first_l, bufs_a, bufs_b, core_a, keep_give, kt, ktq, dg, dgq, send, recv):
     space, blk = lax.axis_index("space"), lax.axis_index("blk")
     count = nz * NXC
     z, x = space // NXC, space % NXC
@@ -244,7 +244,6 @@
     owner = base + (1 - high) * (3 - b4) + high * (b4 - 2)
     b_x = over_x(gb, rxb)
     b_x += [push(keep_give.at[(x + d) % NXC], rxb.at[3 + d], at(0, d, owner)) for d in range(NXC)]
-    rest = push(x_ref, xq, peer_y)
 
     steps = boxes // 2
     landed(*a_r)
@@ -255,28 +254,29 @@
         total = total + rxb[j]
     sb[...] = total
     b_z = over_z(sb, rzb)
+    rest = push(x_ref, xq, peer_y)
     landed(*a_r)
     a_r = ring_step(2, ta, ringa, boxes)
     landed(*b_z)
     tb[...] = sb[z % BOX] + rzb[0] + rzb[1] + rzb[2]
-    b_r = ring_step(0, tb, ringb, boxes)
+    up, far = boxes // 2, 2 * BOX
+    b_far = [push(tb, ringb.at[1], at(far)), push(tb, ringb.at[up + 1], at(-far))]
+    b_r = [push(tb, ringb.at[0], at(BOX)), push(tb, ringb.at[up], at(-BOX))]
     landed(*a_r)
     a_r = ring_step(3, ta, ringa, boxes)
-    landed(*b_r)
-    b_r = ring_step(1, tb, ringb, boxes)
     landed(*a_r)
     total = ta[...]
     for j in range(boxes - 1):
         total = total + ringa[j]
     gza[z % BOX] = total
     a_g = back_z(gza.at[z % BOX], gza)
-    landed(*b_r)
-    b_r = ring_step(2, tb, ringb, boxes)
+    landed(*b_far)
+    b_r.append(push(ringb.at[1], ringb.at[3], at(far)))
+    b_r.append(push(ringb.at[1], ringb.at[2], at(BOX)))
+    b_r.append(push(ringb.at[up + 1], ringb.at[up + 2], at(-BOX)))
     landed(*a_g)
     fa[x] = gza[...]
     a_g = [push(fa.at[x], fa.at[x], at(0, d)) for d in range(1, NXC)]
-    landed(*b_r)
-    b_r = ring_step(3, tb, ringb, boxes)
     landed(*a_g)
     a_c = push(fa, core_a, core)
     landed(*b_r)
@@ -311,13 +311,14 @@
     sign = jnp.where(low == 1, 1.0, -1.0)
     keep_m, take_m = rotation(column(own_a), diag_row(peer_a), own_c, sign, serve)
     pair = jnp.concatenate([keep_m, take_m], axis=0)
+    kt[...] = pair
+    turn = push(kt, ktq, peer_y)
     full = jnp.concatenate(
         [jnp.concatenate([own_a, own_c], axis=1), jnp.concatenate([peer_c, peer_a], axis=1)], axis=0
     )
     own_diag = jnp.sum(pair * mul(full, pair), axis=0, keepdims=True)
-    kt[: 2 * WIDTH] = pair
-    kt[2 * WIDTH :] = jnp.broadcast_to(own_diag, (8, WIDTH))
-    turn = push(kt, ktq, peer_y)
+    dg[...] = jnp.broadcast_to(own_diag, (8, WIDTH))
+    turn_d = push(dg, dgq, peer_y)
 
     def wide(pair):
         ph, plow = halves(pair)
@@ -331,8 +332,7 @@
 
     own_wide = wide(pair)
     landed(turn)
-    pair_q = ktq[: 2 * WIDTH]
-    diag_q = ktq[2 * WIDTH : 2 * WIDTH + 1]
+    pair_q = ktq[...]
     peer_wide = wide(pair_q)
     landed(*spread)
     top = jnp.concatenate([fb[low].reshape(square), fb[2 + low].reshape(square)], axis=1)
@@ -342,7 +342,8 @@
     right = jnp.where(high == 0, pair_q, pair)
     turned = mul(left, mul(cross, right), ROWS_IN)
     turned = jnp.where(high == 0, turned, turned.T)
-    landed(*moved)
+    landed(*moved, turn_d)
+    diag_q = dgq[:1]
 
     def first_round(step):
         i = step // 2
@@ -416,8 +417,10 @@
             sums(7, trail_b, (GROUP,)),
             pltpu.VMEM((NXC, BOX) + trail_a, F32),
             pltpu.VMEM((NXC, BOX) + trail_b, F32),
-            pltpu.VMEM((2 * WIDTH + 8, WIDTH), F32),
-            pltpu.VMEM((2 * WIDTH + 8, WIDTH), F32),
+            pltpu.VMEM((2 * WIDTH, WIDTH), F32),
+            pltpu.VMEM((2 * WIDTH, WIDTH), F32),
+            pltpu.VMEM((8, WIDTH), F32),
+            pltpu.VMEM((8, WIDTH), F32),
             pltpu.SemaphoreType.DMA((80,)),
             pltpu.SemaphoreType.DMA((80,)),
         ],

time: 91.1 us -> 90.9 us (level)
  no operation moved by 1% of the time
where the time goes in v4:
time: 90.9 us; the launch traced here: 90.7 us
  Pallas kernels  88.5 us (97%)
  local copies, waits for them, and re-layouts  2.2 us (2%)
    pallas_call x1, Pallas kernels, rotate(): pl.pallas_call(functools.partial(kernel, nz), out_shape=jax.ShapeDtypeStr...  88.5 us
    unnamed x3, local copies, waits for them, and re-layouts  2.2 us

profile of v4, /device:TPU:1, one launch (start us, length us, event | category | flops | bytes accessed | tf_op | source)
XLA Modules:
  0.0 90.7 jit_solution(16225760753510480187)
XLA Ops:
  0.0 0.0 copy-start
  0.0 1.2 %copy-done = f32[8,16,16,128]{3,2,1,0:T(8,128)S(1)} copy-done((f32[8,16,16,128]{3,2,1,0:T(8,128)S(1)}, f32[8,16,16,128]{3,2,1,0:T(8,128)}, u32[]{:S(2)}) %copy-start) | copy-done | bytes 1048600
  1.2 88.5 %shard_map.17 = f32[8,256,128]{2,1,0:T(8,128)S(1)} custom-call(f32[8,256,128]{2,1,0:T(8,128)S(1)} %bitcast.3), custom_call_target="tpu_custom_call" | custom-call | tf_op jit(solution)/shard_map/pallas_call | solution.py:394
  89.8 1.0 %copy.3 = f32[8,16,16,128]{3,2,1,0:T(8,128)} copy(f32[8,16,16,128]{3,2,1,0:T(8,128)S(1)} %bitcast.2) | data formatting | bytes 2097152
Async XLA Ops:
  0.0 1.2 %copy-start = (f32[8,16,16,128]{3,2,1,0:T(8,128)S(1)}, f32[8,16,16,128]{3,2,1,0:T(8,128)}, u32[]{:S(2)}) copy-start(f32[8,16,16,128]{3,2,1,0:T(8,128)} %param.1) | copy-start | bytes 3145732

commit v5 on v3

--- a/solution.py
+++ b/solution.py
@@ -92,7 +92,7 @@
     return 2.0 * inverse - eye, (2.0 * parity) * solved.T
 
 
-def kernel(nz, x_ref, out_ref, xp, xq, xq1, halo, w, wp, out_half, in_half, xh, xl, xph, xpl, wh, wl, first_h, first_l, bufs_a, bufs_b, core_a, keep_give, kt, ktq, send, recv):
+def kernel(nz, x_hbm, out_ref, x_ref, xp, xq, xq1, halo, w, wp, out_half, in_half, xh, xl, xph, xpl, wh, wl, first_h, first_l, bufs_a, bufs_b, core_a, keep_give, kt, ktq, send, recv):
     space, blk = lax.axis_index("space"), lax.axis_index("blk")
     count = nz * NXC
     z, x = space // NXC, space % NXC
@@ -131,10 +131,13 @@
         for copy in some:
             copy.wait_recv()
 
+    load = pltpu.make_async_copy(x_hbm, x_ref, recv.at[79])
+    load.start()
     barrier = pltpu.get_barrier_semaphore()
     peers = group + rings + [after, before]
     for device in peers:
         pl.semaphore_signal(barrier, inc=1, device_id=device, device_id_type=MESH)
+    load.wait()
     there, here = (1 - high) * half, high * half
     rows = x_ref.shape[1]
     side = rows // 16
@@ -393,9 +396,10 @@
     return pl.pallas_call(
         functools.partial(kernel, nz),
         out_shape=jax.ShapeDtypeStruct(block.shape, F32),
-        in_specs=[pl.BlockSpec(memory_space=pltpu.VMEM)],
+        in_specs=[pl.BlockSpec(memory_space=pl.ANY)],
         out_specs=pl.BlockSpec(memory_space=pltpu.VMEM),
         scratch_shapes=[
+            full,
             full,
             full,
             full,

time: 91.1 us -> 91.2 us (level)
  no operation moved by 1% of the time
where the time goes in v5:
time: 91.2 us; the launch traced here: 91.1 us
  Pallas kernels  88.9 us (97%)
  local copies, waits for them, and re-layouts  2.2 us (2%)
    pallas_call x1, Pallas kernels, rotate(): pl.pallas_call(functools.partial(kernel, nz), out_shape=jax.ShapeDtypeStr...  88.9 us
    unnamed x3, local copies, waits for them, and re-layouts  2.2 us

profile of v5, /device:TPU:1, one launch (start us, length us, event | category | flops | bytes accessed | tf_op | source)
XLA Modules:
  0.0 91.1 jit_solution(13827828406610897243)
XLA Ops:
  0.0 0.0 copy-start
  0.0 1.2 %copy-done = f32[8,16,16,128]{3,2,1,0:T(8,128)S(1)} copy-done((f32[8,16,16,128]{3,2,1,0:T(8,128)S(1)}, f32[8,16,16,128]{3,2,1,0:T(8,128)}, u32[]{:S(2)}) %copy-start) | copy-done | bytes 1048600
  1.2 88.9 %shard_map.17 = f32[8,256,128]{2,1,0:T(8,128)S(1)} custom-call(f32[8,256,128]{2,1,0:T(8,128)S(1)} %bitcast.3), custom_call_target="tpu_custom_call" | custom-call | tf_op jit(solution)/shard_map/pallas_call | solution.py:396
  90.1 1.0 %copy.3 = f32[8,16,16,128]{3,2,1,0:T(8,128)} copy(f32[8,16,16,128]{3,2,1,0:T(8,128)S(1)} %bitcast.2) | data formatting | bytes 2097152
Async XLA Ops:
  0.0 1.2 %copy-start = (f32[8,16,16,128]{3,2,1,0:T(8,128)S(1)}, f32[8,16,16,128]{3,2,1,0:T(8,128)}, u32[]{:S(2)}) copy-start(f32[8,16,16,128]{3,2,1,0:T(8,128)} %param.1) | copy-start | bytes 3145732
